TPU v7x, 512 devices: a whole 4x8x8 slice. The times are simulated.
512 devices in a mesh: row: 16 (over x, z_hi), col: 16 (over y, z_lo), layer: 2 (over core).
Axes of the slice: x: 4, y: 8, z: 8 (z_hi: 4, z_lo: 2; z = z_hi * 2 + z_lo), core: 2. Of those that a mesh axis runs over, the one named last changes fastest.
Arguments:
- matrix: float32 [8192, 8192], P('row', 'col'), may hold values from -1 to 1
- band_cols: int32 [64, 17], replicated, may hold values from 0 to 63, as said below
Outputs:
- new_sign: float32 [8192, 8192], P('row', ('col', 'layer'))
- square: float32 [8192, 8192], P('row', ('col', 'layer'))
Inputs may be any that keep to these rules, and one draw needn't show every extreme that they name: `band_cols`: row p lists 17 different block columns, p itself among them, each q with |q - p| <= 16; the band does not wrap around.
All inputs are finite; a program needn't handle non-finite values.
Results may differ from a plain program's by a relative error of at most 0.0048.
Values may be sent and summed in bfloat16 or wider, within the bound.
A program may use at most 64 MiB of HBM per device.

v0:
```python
import jax
import jax.numpy as jnp
from jax import lax
from jax.sharding import PartitionSpec as P

BLOCK = 128


def passed_along(value, axis, by):
    size = lax.axis_size(axis)
    return lax.ppermute(value, axis, [(i, (i + by) % size) for i in range(size)])


def expand(blocks, size):
    count = blocks.shape[0]
    return jnp.broadcast_to(blocks[:, None, :, None], (count, size, count, size)).reshape(
        count * size, count * size
    )


def skew_cols(values, amount, levels):
    for level in range(levels):
        moved = passed_along(values, "col", -(1 << level))
        values = jnp.where(amount // (1 << level) % 2 == 1, moved, values)
    return values


def skew_rows(values, amount, levels):
    for level in range(levels):
        moved = passed_along(values, "row", -(1 << level))
        values = jnp.where(amount // (1 << level) % 2 == 1, moved, values)
    return values


def next_rows(values):
    return passed_along(values, "row", -1)


def accumulate(total, left, right):
    return total + jnp.dot(left, right, preferred_element_type=jnp.float32)


def per_device(matrix, band_cols):
    side = lax.axis_size("col")
    depth = lax.axis_size("layer")
    half = side // depth
    levels = side.bit_length() - 1
    grid_row = lax.axis_index("row")
    grid_col = lax.axis_index("col")
    layer_index = lax.axis_index("layer")
    tile = matrix.shape[0]
    count = tile // BLOCK
    width = tile // depth
    nblocks = band_cols.shape[0]
    pattern = jnp.any(
        band_cols[:, :, None] == jnp.arange(nblocks, dtype=jnp.int32)[None, None, :], axis=1
    ).astype(jnp.float32)
    own_tile = lax.dynamic_slice(pattern, (grid_row * count, grid_col * count), (count, count))
    mask = expand(own_tile, BLOCK)
    sparse = matrix * mask
    lower = sparse.astype(jnp.bfloat16)
    mask_half = lax.dynamic_slice_in_dim(mask, layer_index * width, width, 1)
    sparse_half = lax.dynamic_slice_in_dim(sparse, layer_index * width, width, 1)
    start = (grid_row + grid_col + half * layer_index) % side
    row_amount = (grid_row + half * layer_index) % side
    col_amount = (grid_col + half * layer_index) % side
    products = jnp.zeros((tile, tile), jnp.float32)
    panels = []
    inners = []
    moving = skew_cols(lower, row_amount, levels)
    right = skew_rows(lower, col_amount, levels)
    for step in range(half):
        inner = (start + step) % side
        panels.append(moving)
        inners.append(inner)
        products = accumulate(products, moving, right)
        if step + 1 < half:
            moving = passed_along(moving, "col", -1)
            right = next_rows(right)
    summed = lax.psum(products, "layer") * mask
    square = lax.dynamic_slice_in_dim(summed, layer_index * width, width, 1)
    square_low = summed.astype(jnp.bfloat16)
    cubes = jnp.zeros((tile, tile), jnp.float32)
    right = skew_rows(square_low, col_amount, levels)
    for step in range(half):
        cubes = accumulate(cubes, panels[step], right)
        if step + 1 < half:
            right = next_rows(right)
    share = lax.psum_scatter(cubes, "layer", scatter_dimension=1, tiled=True)
    new_sign = mask_half * (1.5 * sparse_half - 0.5 * share)
    return (new_sign, square)


def solution(mesh):
    in_specs = (P("row", "col"), P())
    out_specs = (P("row", ("col", "layer")), P("row", ("col", "layer")))
    return jax.shard_map(
        per_device, mesh=mesh, in_specs=in_specs, out_specs=out_specs, check_vma=False
    )
```

profile of v0, /device:TPU:1, one launch (start us, length us, event | category | flops | bytes accessed | tf_op | source)
XLA Modules:
  0.0 732.1 jit_solution(10024606451207785913)
XLA Ops:
  17.3 12.0 %collective-permute-start.4 = (bf16[512,512]{1,0:T(8,128)(2,1)S(1)}, bf16[512,512]{1,0:T(8,128)(2,1)}, u32[]{:S(2)}, u32[]{:S(2)}) collective-permute-start(bf16[512,512]{1,0:T(8,128)(2,1)S(1)} %get-tuple-element.4), channel_id=1, source_target_pairs={{0,480},{32,0},{64,32},{96,64},{128,96},{160,128},{192,160},{224,1... | collective-permute-start | bytes 1572872 | tf_op jit(solution)/shard_map/ppermute | solution.py:11
  30.2 20.7 %collective-permute-done.4 = bf16[512,512]{1,0:T(8,128)(2,1)} collective-permute-done((bf16[512,512]{1,0:T(8,128)(2,1)S(1)}, bf16[512,512]{1,0:T(8,128)(2,1)}, u32[]{:S(2)}, u32[]{:S(2)}) %collective-permute-start.4) | collective-permute-done | bytes 524320 | tf_op jit(solution)/shard_map/ppermute | solution.py:11
  56.0 13.4 %collective-permute-done.5 = bf16[512,512]{1,0:T(8,128)(2,1)} collective-permute-done((bf16[512,512]{1,0:T(8,128)(2,1)}, bf16[512,512]{1,0:T(8,128)(2,1)}, u32[]{:S(2)}, u32[]{:S(2)}) %collective-permute-start.5) | collective-permute-done | bytes 524320 | tf_op jit(solution)/shard_map/ppermute | solution.py:11
  92.6 11.3 %collective-permute-start.3 = (bf16[512,512]{1,0:T(8,128)(2,1)S(1)}, bf16[512,512]{1,0:T(8,128)(2,1)}, u32[]{:S(2)}, u32[]{:S(2)}) collective-permute-start(bf16[512,512]{1,0:T(8,128)(2,1)S(1)} %broadcast_select_fusion.10), channel_id=1, source_target_pairs={{0,16},{2,18},{4,20},{6,22},{8,24},{10,26},{12,28},{14,30},{16,0},... | collective-permute-start | bytes 1572872 | tf_op jit(solution)/shard_map/ppermute | solution.py:11
  105.1 23.4 %collective-permute-start.9 = (bf16[512,512]{1,0:T(8,128)(2,1)S(1)}, bf16[512,512]{1,0:T(8,128)(2,1)S(1)}, u32[]{:S(2)}, u32[]{:S(2)}) collective-permute-start(bf16[512,512]{1,0:T(8,128)(2,1)S(1)} %broadcast_select_fusion.7), channel_id=1, source_target_pairs={{0,480},{32,0},{64,32},{96,64},{128,96},{160,128},{192,160},{224,1... | collective-permute-start | bytes 1572872 | tf_op jit(solution)/shard_map/ppermute | solution.py:11
  193.5 25.1 %collective-permute-start.15 = (bf16[512,512]{1,0:T(8,128)(2,1)S(1)}, bf16[512,512]{1,0:T(8,128)(2,1)S(1)}, u32[]{:S(2)}, u32[]{:S(2)}) collective-permute-start(bf16[512,512]{1,0:T(8,128)(2,1)S(1)} %collective-permute-done.13), channel_id=1, source_target_pairs={{0,480},{32,0},{64,32},{96,64},{128,96},{160,128},{192,160},{224,1... | collective-permute-start | bytes 1572872 | tf_op jit(solution)/shard_map/ppermute | solution.py:11
  237.0 15.7 %collective-permute-start.17 = (bf16[512,512]{1,0:T(8,128)(2,1)S(1)}, bf16[512,512]{1,0:T(8,128)(2,1)S(1)}, u32[]{:S(2)}, u32[]{:S(2)}) collective-permute-start(bf16[512,512]{1,0:T(8,128)(2,1)S(1)} %collective-permute-done.15), channel_id=1, source_target_pairs={{0,480},{32,0},{64,32},{96,64},{128,96},{160,128},{192,160},{224,1... | collective-permute-start | bytes 1572872 | tf_op jit(solution)/shard_map/ppermute | solution.py:11
  271.3 15.2 %collective-permute-start.19 = (bf16[512,512]{1,0:T(8,128)(2,1)S(1)}, bf16[512,512]{1,0:T(8,128)(2,1)S(1)}, u32[]{:S(2)}, u32[]{:S(2)}) collective-permute-start(bf16[512,512]{1,0:T(8,128)(2,1)S(1)} %collective-permute-done.17), channel_id=1, source_target_pairs={{0,480},{32,0},{64,32},{96,64},{128,96},{160,128},{192,160},{224,1... | collective-permute-start | bytes 1572872 | tf_op jit(solution)/shard_map/ppermute | solution.py:11
  303.8 15.9 %collective-permute-start.21 = (bf16[512,512]{1,0:T(8,128)(2,1)S(1)}, bf16[512,512]{1,0:T(8,128)(2,1)S(1)}, u32[]{:S(2)}, u32[]{:S(2)}) collective-permute-start(bf16[512,512]{1,0:T(8,128)(2,1)S(1)} %collective-permute-done.19), channel_id=1, source_target_pairs={{0,480},{32,0},{64,32},{96,64},{128,96},{160,128},{192,160},{224,1... | collective-permute-start | bytes 1572872 | tf_op jit(solution)/shard_map/ppermute | solution.py:11
  337.0 13.4 %collective-permute-done.20 = bf16[512,512]{1,0:T(8,128)(2,1)S(1)} collective-permute-done((bf16[512,512]{1,0:T(8,128)(2,1)S(1)}, bf16[512,512]{1,0:T(8,128)(2,1)S(1)}, u32[]{:S(2)}, u32[]{:S(2)}) %collective-permute-start.20) | collective-permute-done | bytes 524320 | tf_op jit(solution)/shard_map/ppermute | solution.py:11
  352.7 61.0 %all-reduce.2.cloned.1.call-done = f32[512,512]{1,0:T(8,128)} async-done(((f32[512,512]{1,0:T(8,128)}), f32[512,512]{1,0:T(8,128)}) %all-reduce.2.cloned.1.call-update) | async-done | bytes 1048592 | tf_op jit(solution)/shard_map/psum | solution.py:80
  423.5 22.5 %collective-permute-done.22 = bf16[512,512]{1,0:T(8,128)(2,1)S(1)} collective-permute-done((bf16[512,512]{1,0:T(8,128)(2,1)S(1)}, bf16[512,512]{1,0:T(8,128)(2,1)S(1)}, u32[]{:S(2)}, u32[]{:S(2)}) %collective-permute-start.22) | collective-permute-done | bytes 524320 | tf_op jit(solution)/shard_map/ppermute | solution.py:11
  452.7 11.8 %collective-permute-done.23 = bf16[512,512]{1,0:T(8,128)(2,1)S(1)} collective-permute-done((bf16[512,512]{1,0:T(8,128)(2,1)S(1)}, bf16[512,512]{1,0:T(8,128)(2,1)S(1)}, u32[]{:S(2)}, u32[]{:S(2)}) %collective-permute-start.23) | collective-permute-done | bytes 524320 | tf_op jit(solution)/shard_map/ppermute | solution.py:11
  467.2 10.9 %collective-permute-done.24 = bf16[512,512]{1,0:T(8,128)(2,1)S(1)} collective-permute-done((bf16[512,512]{1,0:T(8,128)(2,1)S(1)}, bf16[512,512]{1,0:T(8,128)(2,1)S(1)}, u32[]{:S(2)}, u32[]{:S(2)}) %collective-permute-start.24) | collective-permute-done | bytes 524320 | tf_op jit(solution)/shard_map/ppermute | solution.py:11
  480.7 11.5 %collective-permute-done.25 = bf16[512,512]{1,0:T(8,128)(2,1)S(1)} collective-permute-done((bf16[512,512]{1,0:T(8,128)(2,1)S(1)}, bf16[512,512]{1,0:T(8,128)(2,1)S(1)}, u32[]{:S(2)}, u32[]{:S(2)}) %collective-permute-start.25) | collective-permute-done | bytes 524320 | tf_op jit(solution)/shard_map/ppermute | solution.py:11
  492.2 25.7 %collective-permute-start.26 = (bf16[512,512]{1,0:T(8,128)(2,1)S(1)}, bf16[512,512]{1,0:T(8,128)(2,1)S(1)}, u32[]{:S(2)}, u32[]{:S(2)}) collective-permute-start(bf16[512,512]{1,0:T(8,128)(2,1)S(1)} %broadcast_select_fusion.6), channel_id=1, source_target_pairs={{0,480},{32,0},{64,32},{96,64},{128,96},{160,128},{192,160},{224,1... | collective-permute-start | bytes 1572872 | tf_op jit(solution)/shard_map/ppermute | solution.py:11
  517.9 12.5 %collective-permute-done.26 = bf16[512,512]{1,0:T(8,128)(2,1)S(1)} collective-permute-done((bf16[512,512]{1,0:T(8,128)(2,1)S(1)}, bf16[512,512]{1,0:T(8,128)(2,1)S(1)}, u32[]{:S(2)}, u32[]{:S(2)}) %collective-permute-start.26) | collective-permute-done | bytes 524320 | tf_op jit(solution)/shard_map/ppermute | solution.py:11
  537.5 15.4 %collective-permute-done.27 = bf16[512,512]{1,0:T(8,128)(2,1)S(1)} collective-permute-done((bf16[512,512]{1,0:T(8,128)(2,1)S(1)}, bf16[512,512]{1,0:T(8,128)(2,1)S(1)}, u32[]{:S(2)}, u32[]{:S(2)}) %collective-permute-start.27) | collective-permute-done | bytes 524320 | tf_op jit(solution)/shard_map/ppermute | solution.py:11
  554.8 13.8 %collective-permute-done.28 = bf16[512,512]{1,0:T(8,128)(2,1)S(1)} collective-permute-done((bf16[512,512]{1,0:T(8,128)(2,1)S(1)}, bf16[512,512]{1,0:T(8,128)(2,1)S(1)}, u32[]{:S(2)}, u32[]{:S(2)}) %collective-permute-start.28) | collective-permute-done | bytes 524320 | tf_op jit(solution)/shard_map/ppermute | solution.py:11
  576.3 18.3 %collective-permute-done.29 = bf16[512,512]{1,0:T(8,128)(2,1)S(1)} collective-permute-done((bf16[512,512]{1,0:T(8,128)(2,1)S(1)}, bf16[512,512]{1,0:T(8,128)(2,1)S(1)}, u32[]{:S(2)}, u32[]{:S(2)}) %collective-permute-start.29) | collective-permute-done | bytes 524320 | tf_op jit(solution)/shard_map/ppermute | solution.py:11
  603.5 18.2 %collective-permute-done.30 = bf16[512,512]{1,0:T(8,128)(2,1)S(1)} collective-permute-done((bf16[512,512]{1,0:T(8,128)(2,1)S(1)}, bf16[512,512]{1,0:T(8,128)(2,1)S(1)}, u32[]{:S(2)}, u32[]{:S(2)}) %collective-permute-start.30) | collective-permute-done | bytes 524320 | tf_op jit(solution)/shard_map/ppermute | solution.py:11
  629.5 19.3 %collective-permute-done.31 = bf16[512,512]{1,0:T(8,128)(2,1)S(1)} collective-permute-done((bf16[512,512]{1,0:T(8,128)(2,1)S(1)}, bf16[512,512]{1,0:T(8,128)(2,1)S(1)}, u32[]{:S(2)}, u32[]{:S(2)}) %collective-permute-start.31) | collective-permute-done | bytes 524320 | tf_op jit(solution)/shard_map/ppermute | solution.py:11
  654.4 21.3 %collective-permute-done.32 = bf16[512,512]{1,0:T(8,128)(2,1)S(1)} collective-permute-done((bf16[512,512]{1,0:T(8,128)(2,1)S(1)}, bf16[512,512]{1,0:T(8,128)(2,1)S(1)}, u32[]{:S(2)}, u32[]{:S(2)}) %collective-permute-start.32) | collective-permute-done | bytes 524320 | tf_op jit(solution)/shard_map/ppermute | solution.py:11
  679.6 43.7 %reduce-scatter.2.cloned.1.call-done = f32[512,256]{1,0:T(8,128)} async-done(((f32[512,512]{1,0:T(8,128)}), f32[512,256]{1,0:T(8,128)}) %reduce-scatter.2.cloned.1.call-update) | async-done | bytes 524304 | tf_op jit(solution)/shard_map/reduce_scatter | solution.py:89
  (119 shorter events, 245.4 us)
Async XLA Ops:
  7.2 406.5 %all-reduce.2.cloned.1.call-start = ((), (), s32[]{:S(2)}) async-start(), calls=%async_computation.1 | async-start | bytes 2097152 | tf_op jit(solution)/shard_map/psum | solution.py:80
  17.3 33.5 %collective-permute-start.4 = (bf16[512,512]{1,0:T(8,128)(2,1)S(1)}, bf16[512,512]{1,0:T(8,128)(2,1)}, u32[]{:S(2)}, u32[]{:S(2)}) collective-permute-start(bf16[512,512]{1,0:T(8,128)(2,1)S(1)} %get-tuple-element.4), channel_id=1, source_target_pairs={{0,480},{32,0},{64,32},{96,64},{128,96},{160,128},{192,160},{224,1... | collective-permute-start | bytes 1572872 | tf_op jit(solution)/shard_map/ppermute | solution.py:11
  92.6 35.9 %collective-permute-start.3 = (bf16[512,512]{1,0:T(8,128)(2,1)S(1)}, bf16[512,512]{1,0:T(8,128)(2,1)}, u32[]{:S(2)}, u32[]{:S(2)}) collective-permute-start(bf16[512,512]{1,0:T(8,128)(2,1)S(1)} %broadcast_select_fusion.10), channel_id=1, source_target_pairs={{0,16},{2,18},{4,20},{6,22},{8,24},{10,26},{12,28},{14,30},{16,0},... | collective-permute-start | bytes 1572872 | tf_op jit(solution)/shard_map/ppermute | solution.py:11
  105.1 39.0 %collective-permute-start.9 = (bf16[512,512]{1,0:T(8,128)(2,1)S(1)}, bf16[512,512]{1,0:T(8,128)(2,1)S(1)}, u32[]{:S(2)}, u32[]{:S(2)}) collective-permute-start(bf16[512,512]{1,0:T(8,128)(2,1)S(1)} %broadcast_select_fusion.7), channel_id=1, source_target_pairs={{0,480},{32,0},{64,32},{96,64},{128,96},{160,128},{192,160},{224,1... | collective-permute-start | bytes 1572872 | tf_op jit(solution)/shard_map/ppermute | solution.py:11
  129.7 22.7 %collective-permute-start.8 = (bf16[512,512]{1,0:T(8,128)(2,1)S(1)}, bf16[512,512]{1,0:T(8,128)(2,1)S(1)}, u32[]{:S(2)}, u32[]{:S(2)}) collective-permute-start(bf16[512,512]{1,0:T(8,128)(2,1)S(1)} %broadcast_select_fusion.11), channel_id=1, source_target_pairs={{0,30},{2,0},{4,2},{6,4},{8,6},{10,8},{12,10},{14,12},{16,14},{18,... | collective-permute-start | bytes 1572872 | tf_op jit(solution)/shard_map/ppermute | solution.py:11
  144.1 25.8 %collective-permute-start.11 = (bf16[512,512]{1,0:T(8,128)(2,1)S(1)}, bf16[512,512]{1,0:T(8,128)(2,1)S(1)}, u32[]{:S(2)}, u32[]{:S(2)}) collective-permute-start(bf16[512,512]{1,0:T(8,128)(2,1)S(1)} %collective-permute-done.9), channel_id=1, source_target_pairs={{0,480},{32,0},{64,32},{96,64},{128,96},{160,128},{192,160},{224,1... | collective-permute-start | bytes 1572872 | tf_op jit(solution)/shard_map/ppermute | solution.py:11
  152.4 34.9 %collective-permute-start.10 = (bf16[512,512]{1,0:T(8,128)(2,1)S(1)}, bf16[512,512]{1,0:T(8,128)(2,1)S(1)}, u32[]{:S(2)}, u32[]{:S(2)}) collective-permute-start(bf16[512,512]{1,0:T(8,128)(2,1)S(1)} %collective-permute-done.8), channel_id=1, source_target_pairs={{0,30},{2,0},{4,2},{6,4},{8,6},{10,8},{12,10},{14,12},{16,14},{18,... | collective-permute-start | bytes 1572872 | tf_op jit(solution)/shard_map/ppermute | solution.py:11
  169.9 23.6 %collective-permute-start.13 = (bf16[512,512]{1,0:T(8,128)(2,1)S(1)}, bf16[512,512]{1,0:T(8,128)(2,1)S(1)}, u32[]{:S(2)}, u32[]{:S(2)}) collective-permute-start(bf16[512,512]{1,0:T(8,128)(2,1)S(1)} %collective-permute-done.11), channel_id=1, source_target_pairs={{0,480},{32,0},{64,32},{96,64},{128,96},{160,128},{192,160},{224,1... | collective-permute-start | bytes 1572872 | tf_op jit(solution)/shard_map/ppermute | solution.py:11
  187.3 33.7 %collective-permute-start.12 = (bf16[512,512]{1,0:T(8,128)(2,1)S(1)}, bf16[512,512]{1,0:T(8,128)(2,1)S(1)}, u32[]{:S(2)}, u32[]{:S(2)}) collective-permute-start(bf16[512,512]{1,0:T(8,128)(2,1)S(1)} %collective-permute-done.10), channel_id=1, source_target_pairs={{0,30},{2,0},{4,2},{6,4},{8,6},{10,8},{12,10},{14,12},{16,14},{18,... | collective-permute-start | bytes 1572872 | tf_op jit(solution)/shard_map/ppermute | solution.py:11
  193.5 43.5 %collective-permute-start.15 = (bf16[512,512]{1,0:T(8,128)(2,1)S(1)}, bf16[512,512]{1,0:T(8,128)(2,1)S(1)}, u32[]{:S(2)}, u32[]{:S(2)}) collective-permute-start(bf16[512,512]{1,0:T(8,128)(2,1)S(1)} %collective-permute-done.13), channel_id=1, source_target_pairs={{0,480},{32,0},{64,32},{96,64},{128,96},{160,128},{192,160},{224,1... | collective-permute-start | bytes 1572872 | tf_op jit(solution)/shard_map/ppermute | solution.py:11
  221.0 33.7 %collective-permute-start.14 = (bf16[512,512]{1,0:T(8,128)(2,1)S(1)}, bf16[512,512]{1,0:T(8,128)(2,1)S(1)}, u32[]{:S(2)}, u32[]{:S(2)}) collective-permute-start(bf16[512,512]{1,0:T(8,128)(2,1)S(1)} %collective-permute-done.12), channel_id=1, source_target_pairs={{0,30},{2,0},{4,2},{6,4},{8,6},{10,8},{12,10},{14,12},{16,14},{18,... | collective-permute-start | bytes 1572872 | tf_op jit(solution)/shard_map/ppermute | solution.py:11
  237.0 34.3 %collective-permute-start.17 = (bf16[512,512]{1,0:T(8,128)(2,1)S(1)}, bf16[512,512]{1,0:T(8,128)(2,1)S(1)}, u32[]{:S(2)}, u32[]{:S(2)}) collective-permute-start(bf16[512,512]{1,0:T(8,128)(2,1)S(1)} %collective-permute-done.15), channel_id=1, source_target_pairs={{0,480},{32,0},{64,32},{96,64},{128,96},{160,128},{192,160},{224,1... | collective-permute-start | bytes 1572872 | tf_op jit(solution)/shard_map/ppermute | solution.py:11
  254.7 33.8 %collective-permute-start.16 = (bf16[512,512]{1,0:T(8,128)(2,1)S(1)}, bf16[512,512]{1,0:T(8,128)(2,1)S(1)}, u32[]{:S(2)}, u32[]{:S(2)}) collective-permute-start(bf16[512,512]{1,0:T(8,128)(2,1)S(1)} %collective-permute-done.14), channel_id=1, source_target_pairs={{0,30},{2,0},{4,2},{6,4},{8,6},{10,8},{12,10},{14,12},{16,14},{18,... | collective-permute-start | bytes 1572872 | tf_op jit(solution)/shard_map/ppermute | solution.py:11
  271.3 32.6 %collective-permute-start.19 = (bf16[512,512]{1,0:T(8,128)(2,1)S(1)}, bf16[512,512]{1,0:T(8,128)(2,1)S(1)}, u32[]{:S(2)}, u32[]{:S(2)}) collective-permute-start(bf16[512,512]{1,0:T(8,128)(2,1)S(1)} %collective-permute-done.17), channel_id=1, source_target_pairs={{0,480},{32,0},{64,32},{96,64},{128,96},{160,128},{192,160},{224,1... | collective-permute-start | bytes 1572872 | tf_op jit(solution)/shard_map/ppermute | solution.py:11
  288.5 33.7 %collective-permute-start.18 = (bf16[512,512]{1,0:T(8,128)(2,1)S(1)}, bf16[512,512]{1,0:T(8,128)(2,1)S(1)}, u32[]{:S(2)}, u32[]{:S(2)}) collective-permute-start(bf16[512,512]{1,0:T(8,128)(2,1)S(1)} %collective-permute-done.16), channel_id=1, source_target_pairs={{0,30},{2,0},{4,2},{6,4},{8,6},{10,8},{12,10},{14,12},{16,14},{18,... | collective-permute-start | bytes 1572872 | tf_op jit(solution)/shard_map/ppermute | solution.py:11
  303.8 33.1 %collective-permute-start.21 = (bf16[512,512]{1,0:T(8,128)(2,1)S(1)}, bf16[512,512]{1,0:T(8,128)(2,1)S(1)}, u32[]{:S(2)}, u32[]{:S(2)}) collective-permute-start(bf16[512,512]{1,0:T(8,128)(2,1)S(1)} %collective-permute-done.19), channel_id=1, source_target_pairs={{0,480},{32,0},{64,32},{96,64},{128,96},{160,128},{192,160},{224,1... | collective-permute-start | bytes 1572872 | tf_op jit(solution)/shard_map/ppermute | solution.py:11
  322.2 28.1 %collective-permute-start.20 = (bf16[512,512]{1,0:T(8,128)(2,1)S(1)}, bf16[512,512]{1,0:T(8,128)(2,1)S(1)}, u32[]{:S(2)}, u32[]{:S(2)}) collective-permute-start(bf16[512,512]{1,0:T(8,128)(2,1)S(1)} %collective-permute-done.18), channel_id=1, source_target_pairs={{0,30},{2,0},{4,2},{6,4},{8,6},{10,8},{12,10},{14,12},{16,14},{18,... | collective-permute-start | bytes 1572872 | tf_op jit(solution)/shard_map/ppermute | solution.py:11
  352.6 370.7 %reduce-scatter.2.cloned.1.call-start = ((), (), s32[]{:S(2)}) async-start(), calls=%async_computation.2 | async-start | bytes 1572864 | tf_op jit(solution)/shard_map/reduce_scatter | solution.py:89
  416.1 29.9 %collective-permute-start.22 = (bf16[512,512]{1,0:T(8,128)(2,1)S(1)}, bf16[512,512]{1,0:T(8,128)(2,1)S(1)}, u32[]{:S(2)}, u32[]{:S(2)}) collective-permute-start(bf16[512,512]{1,0:T(8,128)(2,1)S(1)} %get-tuple-element.2), channel_id=1, source_target_pairs={{0,480},{32,0},{64,32},{96,64},{128,96},{160,128},{192,160},{224,1... | collective-permute-start | bytes 1572872 | tf_op jit(solution)/shard_map/ppermute | solution.py:11
  492.2 38.2 %collective-permute-start.26 = (bf16[512,512]{1,0:T(8,128)(2,1)S(1)}, bf16[512,512]{1,0:T(8,128)(2,1)S(1)}, u32[]{:S(2)}, u32[]{:S(2)}) collective-permute-start(bf16[512,512]{1,0:T(8,128)(2,1)S(1)} %broadcast_select_fusion.6), channel_id=1, source_target_pairs={{0,480},{32,0},{64,32},{96,64},{128,96},{160,128},{192,160},{224,1... | collective-permute-start | bytes 1572872 | tf_op jit(solution)/shard_map/ppermute | solution.py:11
  568.6 25.9 %collective-permute-start.29 = (bf16[512,512]{1,0:T(8,128)(2,1)S(1)}, bf16[512,512]{1,0:T(8,128)(2,1)S(1)}, u32[]{:S(2)}, u32[]{:S(2)}) collective-permute-start(bf16[512,512]{1,0:T(8,128)(2,1)S(1)} %collective-permute-done.28), channel_id=1, source_target_pairs={{0,480},{32,0},{64,32},{96,64},{128,96},{160,128},{192,160},{224,1... | collective-permute-start | bytes 1572872 | tf_op jit(solution)/shard_map/ppermute | solution.py:11
  594.6 27.1 %collective-permute-start.30 = (bf16[512,512]{1,0:T(8,128)(2,1)S(1)}, bf16[512,512]{1,0:T(8,128)(2,1)S(1)}, u32[]{:S(2)}, u32[]{:S(2)}) collective-permute-start(bf16[512,512]{1,0:T(8,128)(2,1)S(1)} %collective-permute-done.29), channel_id=1, source_target_pairs={{0,480},{32,0},{64,32},{96,64},{128,96},{160,128},{192,160},{224,1... | collective-permute-start | bytes 1572872 | tf_op jit(solution)/shard_map/ppermute | solution.py:11
  621.7 27.1 %collective-permute-start.31 = (bf16[512,512]{1,0:T(8,128)(2,1)S(1)}, bf16[512,512]{1,0:T(8,128)(2,1)S(1)}, u32[]{:S(2)}, u32[]{:S(2)}) collective-permute-start(bf16[512,512]{1,0:T(8,128)(2,1)S(1)} %collective-permute-done.30), channel_id=1, source_target_pairs={{0,480},{32,0},{64,32},{96,64},{128,96},{160,128},{192,160},{224,1... | collective-permute-start | bytes 1572872 | tf_op jit(solution)/shard_map/ppermute | solution.py:11
  648.8 26.9 %collective-permute-start.32 = (bf16[512,512]{1,0:T(8,128)(2,1)S(1)}, bf16[512,512]{1,0:T(8,128)(2,1)S(1)}, u32[]{:S(2)}, u32[]{:S(2)}) collective-permute-start(bf16[512,512]{1,0:T(8,128)(2,1)S(1)} %collective-permute-done.31), channel_id=1, source_target_pairs={{0,480},{32,0},{64,32},{96,64},{128,96},{160,128},{192,160},{224,1... | collective-permute-start | bytes 1572872 | tf_op jit(solution)/shard_map/ppermute | solution.py:11
  (29 other events, 640.3 us)
Sparse Core Ops, SparseCore 0:
  352.7 60.8 all-reduce.1
  677.3 45.9 reduce-scatter.1
where the time goes:
time: 734 us; the launch traced here: 732 us
  waiting for transfers between devices  399 us (54%)
  starting transfers between devices  291 us (40%)
  between operations  15 us (2%)
  other arithmetic  12.5 us (2%)
  matrix products  8.94 us (1%)
    ppermute x33, waiting for transfers between devices, passed_along(): lax.ppermute(value, axis, [(i, (i + by) % size) for i in range(size)])  294 us
    ppermute x33, starting transfers between devices, passed_along(): lax.ppermute(value, axis, [(i, (i + by) % size) for i in range(size)])  291 us
    psum x1, waiting for transfers between devices, per_device(): summed = lax.psum(products, 'layer') * mask  61 us
    reduce_scatter x1, waiting for transfers between devices, per_device(): share = lax.psum_scatter(cubes, 'layer', scatter_dimension=1, tiled=True)  43.7 us
  transfers between devices with their start and end apart: 35, of which 29 were waited for; matrix products, arithmetic and copies ran while one was open for 2% of the time, Pallas kernels for 0%

commit v1 on v0

v1 whole, which is shorter than its diff:
```python
import jax
import jax.numpy as jnp
from jax import lax
from jax.experimental import pallas as pl
from jax.experimental.pallas import tpu as pltpu
from jax.sharding import PartitionSpec as P

BLOCK = 128
REACH = 4
PIECES = 4
MESH = pl.DeviceIdType.MESH


def kernel(band_ref, mat_ref, sign_ref, square_ref, left, right, cube, mask_ref, acc,
           left_recv, sib_recv, right_recv, cube_recv, send_sems):
    r = lax.axis_index("row")
    c = lax.axis_index("col")
    l = lax.axis_index("layer")
    tile = mat_ref.shape[0]
    width = tile // 2
    count = tile // BLOCK
    piece = tile // PIECES
    x, zh = r // 4, r % 4
    y, zl = c // 2, c % 2
    ol = 1 - zl

    def at(dx=0, dzh=0, dy=0, zlow=None):
        zlow = zl if zlow is None else zlow
        return (((x + dx + 4) % 4) * 4 + (zh + dzh + 4) % 4, ((y + dy + 8) % 8) * 2 + zlow, l)

    up, down = at(dy=1), at(dy=-1)
    pair = at(zlow=ol)
    zup, zdown = at(dzh=1), at(dzh=-1)
    xup, xdown = at(dx=1), at(dx=-1)
    sibling = (r, c, 1 - l)

    barrier = pltpu.get_barrier_semaphore()
    for other in (up, down, pair, zup, zdown, xup, xdown, sibling):
        pl.semaphore_signal(barrier, inc=1, device_id=other, device_id_type=MESH)

    column = 4 * c + lax.broadcasted_iota(jnp.int32, (1, tile), 1) // BLOCK
    own_left = 4 + zl
    own_right = 4 + zh
    for a in range(count):
        hit = column == band_ref[count * r + a, 0]
        for j in range(1, band_ref.shape[1]):
            hit = hit | (column == band_ref[count * r + a, j])
        row_mask = jnp.where(hit, 1.0, 0.0).astype(jnp.float32)
        mask_ref[pl.ds(a, 1), :] = row_mask
        rows = pl.ds(a * BLOCK, BLOCK)
        low = (mat_ref[rows, :] * row_mask).astype(jnp.bfloat16)
        left[own_left, 0, rows, :] = low[:, :width]
        left[own_left, 1, rows, :] = low[:, width:]
        right[own_right, rows, :] = left[own_left, l, rows, :]

    pl.semaphore_wait(barrier, 8)

    sent = []

    def send(src, dst, recv_sem, device):
        copy = pltpu.make_async_remote_copy(
            src_ref=src, dst_ref=dst, send_sem=send_sems.at[len(sent)], recv_sem=recv_sem,
            device_id=device, device_id_type=MESH)
        copy.start()
        sent.append(copy)

    def arrived(ref, sem):
        pltpu.make_async_remote_copy(
            src_ref=ref, dst_ref=ref, send_sem=send_sems.at[0], recv_sem=sem,
            device_id=sibling, device_id_type=MESH).wait_recv()

    def part(p):
        return pl.ds(p * piece, piece)

    def send_left(slot, to_slot, p, device):
        send(left.at[slot, l, part(p)], left.at[to_slot, l, part(p)], left_recv.at[to_slot, p], device)

    def wait_left(slot, p):
        arrived(left.at[slot, l, part(p)], left_recv.at[slot, p])
        send(left.at[slot, l, part(p)], left.at[slot, l, part(p)], sib_recv.at[slot, p], sibling)

    def column_start(buf, sem, p):
        src = buf.at[own_right, part(p)]
        send(src, src, sem.at[own_right, p], zup)
        send(src, src, sem.at[own_right, p], zdown)
        send(src, buf.at[zh, part(p)], sem.at[zh, p], xup)
        send(src, buf.at[8 + zh, part(p)], sem.at[8 + zh, p], xdown)

    def along_x(buf, sem, zs, p):
        higher = zs > zh
        slot = jnp.where(higher, zs, 8 + zs)
        device = (jnp.where(higher, xup[0], xdown[0]), c, l)
        send(buf.at[4 + zs, part(p)], buf.at[slot, part(p)], sem.at[slot, p], device)

    def column_near(buf, sem, p):
        for step in (-1, 1):
            zs = (zh + step + 4) % 4
            slot = 4 + zs
            arrived(buf.at[slot, part(p)], sem.at[slot, p])
            if (p < PIECES // 2) == (step == -1):
                send(buf.at[slot, part(p)], buf.at[slot, part(p)], sem.at[slot, p], zup if step == -1 else zdown)
            along_x(buf, sem, zs, p)

    def column_far(buf, sem, p):
        zs = (zh + 2) % 4
        arrived(buf.at[4 + zs, part(p)], sem.at[4 + zs, p])
        along_x(buf, sem, zs, p)

    def column_end(buf, sem):
        for p in range(PIECES):
            arrived(buf.at[zh, part(p)], sem.at[zh, p])
            arrived(buf.at[8 + zh, part(p)], sem.at[8 + zh, p])
            for step in (1, 3, 2):
                zs = (zh + step) % 4
                slot = jnp.where(zs > zh, zs, 8 + zs)
                arrived(buf.at[slot, part(p)], sem.at[slot, p])

    far_src = jnp.where(zl == 0, 3, 6)
    far_dst = jnp.where(zl == 0, 1, 8)
    far_device = (r, jnp.where(zl == 0, up[1], down[1]), l)

    for p in range(PIECES):
        column_start(right, right_recv, p)
        send_left(own_left, 2 + zl, p, up)
        send_left(own_left, 6 + zl, p, down)
        send_left(own_left, own_left, p, pair)
    for p in range(PIECES):
        wait_left(2 + zl, p)
        send_left(2 + zl, zl, p, up)
        wait_left(6 + zl, p)
        send_left(6 + zl, 8 + zl, p, down)
        wait_left(4 + ol, p)
        send_left(4 + ol, 2 + ol, p, up)
        send_left(4 + ol, 6 + ol, p, down)
        column_near(right, right_recv, p)
    for p in range(PIECES):
        wait_left(2 + ol, p)
        wait_left(6 + ol, p)
        send_left(far_src, far_dst, p, far_device)
        column_far(right, right_recv, p)
    for p in range(PIECES):
        wait_left(zl, p)
        wait_left(8 + zl, p)
        wait_left(far_dst, p)
    for p in range(PIECES):
        for slot in (2 + zl, 6 + zl, 4 + ol, 2 + ol, 6 + ol, zl, 8 + zl, far_dst):
            arrived(left.at[slot, 1 - l, part(p)], sib_recv.at[slot, p])
    column_end(right, right_recv)

    first = jnp.maximum(jnp.maximum(r, c) - REACH, 0)
    last = jnp.minimum(jnp.minimum(r, c) + REACH, 15)
    inside = (c - r <= REACH) & (r - c <= REACH)
    stop = jnp.where(inside, last + 1, first)

    def product(buf):
        acc[...] = jnp.zeros_like(acc)

        def body(k, carry):
            ls = k - c + zl + 4
            rs = k - r + zh + 4
            acc[...] += jnp.dot(left[ls, 0], buf[rs, :width, :], preferred_element_type=jnp.float32) + jnp.dot(
                left[ls, 1], buf[rs, width:, :], preferred_element_type=jnp.float32)
            return carry

        lax.fori_loop(first, stop, body, 0)

    half = pl.ds(pl.multiple_of(l * width, width), width)
    product(right)
    for a in range(count):
        rows = pl.ds(a * BLOCK, BLOCK)
        value = acc[rows, :] * mask_ref[pl.ds(a, 1), half]
        square_ref[rows, :] = value
        cube[own_right, rows, :] = value.astype(jnp.bfloat16)

    for p in range(PIECES):
        column_start(cube, cube_recv, p)
    for p in range(PIECES):
        column_near(cube, cube_recv, p)
    for p in range(PIECES):
        column_far(cube, cube_recv, p)
    column_end(cube, cube_recv)

    product(cube)
    for a in range(count):
        rows = pl.ds(a * BLOCK, BLOCK)
        row_mask = mask_ref[pl.ds(a, 1), half]
        sparse = mat_ref[rows, half] * row_mask
        sign_ref[rows, :] = row_mask * (1.5 * sparse - 0.5 * acc[rows, :])

    for copy in sent:
        copy.wait_send()


def per_device(matrix, band_cols):
    tile = matrix.shape[0]
    width = tile // 2
    out = jax.ShapeDtypeStruct((tile, width), jnp.float32)
    return pl.pallas_call(
        kernel,
        out_shape=(out, out),
        in_specs=[pl.BlockSpec(memory_space=pltpu.SMEM), pl.BlockSpec(memory_space=pltpu.VMEM)],
        out_specs=(pl.BlockSpec(memory_space=pltpu.VMEM),) * 2,
        scratch_shapes=[
            pltpu.VMEM((10, 2, tile, width), jnp.bfloat16),
            pltpu.VMEM((12, tile, width), jnp.bfloat16),
            pltpu.VMEM((12, tile, width), jnp.bfloat16),
            pltpu.VMEM((8, tile), jnp.float32),
            pltpu.VMEM((tile, width), jnp.float32),
            pltpu.SemaphoreType.DMA((10, PIECES)),
            pltpu.SemaphoreType.DMA((10, PIECES)),
            pltpu.SemaphoreType.DMA((12, PIECES)),
            pltpu.SemaphoreType.DMA((12, PIECES)),
            pltpu.SemaphoreType.DMA((32 * PIECES,)),
        ],
        compiler_params=pltpu.CompilerParams(
            collective_id=0, has_side_effects=True, vmem_limit_bytes=48 * 2**20),
        cost_estimate=pl.CostEstimate(flops=4 * 10**9, bytes_accessed=2 * 2**20, transcendentals=0),
    )(band_cols, matrix)


def solution(mesh):
    in_specs = (P("row", "col"), P())
    out_specs = (P("row", ("col", "layer")), P("row", ("col", "layer")))
    return jax.shard_map(
        per_device, mesh=mesh, in_specs=in_specs, out_specs=out_specs, check_vma=False
    )
```

time: 734 us -> 84.5 us (0.12)
  waiting for transfers between devices: 399 us -> 0 us
  starting transfers between devices: 291 us -> 0 us
  Pallas kernels: 0 us -> 80.1 us
  between operations: 15 us -> 0.64 us
  other arithmetic: 12.5 us -> 0 us
  matrix products: 8.94 us -> 0 us
    ppermute x33 -> x0, waiting for transfers between devices: 294 us -> none  [passed_along(): lax.ppermute(value, axis, [(i, (i + by) % size) for i in range(size)])]
    ppermute x33 -> x0, starting transfers between devices: 291 us -> none  [passed_along(): lax.ppermute(value, axis, [(i, (i + by) % size) for i in range(size)])]
    pallas_call x0 -> x1, Pallas kernels: none -> 80.1 us  [per_device(): pl.pallas_call(kernel, out_shape=(out, out), in_specs=[pl.BlockSpec(memor...]
    psum x1 -> x0, waiting for transfers between devices: 61 us -> none  [per_device(): summed = lax.psum(products, 'layer') * mask]
    reduce_scatter x1 -> x0, waiting for transfers between devices: 43.7 us -> none  [per_device(): share = lax.psum_scatter(cubes, 'layer', scatter_dimension=1, tiled=True)]
    dot_general x16 -> x0, matrix products: 8.94 us -> none  [accumulate(): return total + jnp.dot(left, right, preferred_element_type=jnp.float32)]
    select_n x11 -> x0, other arithmetic: 7.48 us -> none  [the longest x8 4.41 us: skew_rows(): values = jnp.where(amount // (1 << level) % 2 == 1, moved, values)]
  transfers between devices with their start and end apart: 35 -> 0, of which waited for: 29 -> 0; matrix products, arithmetic and copies ran while one was open for 2% -> 0% of each run, Pallas kernels for 0% -> 0%
where the time goes in v1:
time: 84.5 us; the launch traced here: 84.3 us
  Pallas kernels  80.1 us (95%)
  local copies, waits for them, and re-layouts  3.61 us (4%)
    pallas_call x1, Pallas kernels, per_device(): pl.pallas_call(kernel, out_shape=(out, out), in_specs=[pl.BlockSpec(memor...  80.1 us
    unnamed x5, local copies, waits for them, and re-layouts  3.61 us

profile of v1, /device:TPU:1, one launch (start us, length us, event | category | flops | bytes accessed | tf_op | source)
XLA Modules:
  0.0 84.3 jit_solution(11047912762017159813)
XLA Ops:
  0.6 0.8 copy.4.band_ref
  1.4 0.0 copy-start
  1.4 1.2 %copy-done = f32[512,512]{1,0:T(8,128)S(1)} copy-done((f32[512,512]{1,0:T(8,128)S(1)}, f32[512,512]{1,0:T(8,128)}, u32[]{:S(2)}) %copy-start) | copy-done | bytes 1048600
  2.6 80.1 %shard_map.41 = (f32[512,256]{1,0:T(8,128)S(1)}, f32[512,256]{1,0:T(8,128)S(1)}) custom-call(s32[64,17]{1,0:T(8,128)S(1)} %copy.4.band_ref, f32[512,512]{1,0:T(8,128)S(1)} %copy-done), custom_call_target="tpu_custom_call" | custom-call | flops 4000000000 | bytes 2097152 | tf_op jit(solution)/shard_map/pallas_call | solution.py:198
  82.8 0.8 copy.7
  83.6 0.8 copy.8
Async XLA Ops:
  1.4 1.2 %copy-start = (f32[512,512]{1,0:T(8,128)S(1)}, f32[512,512]{1,0:T(8,128)}, u32[]{:S(2)}) copy-start(f32[512,512]{1,0:T(8,128)} %mat_ref.1) | copy-start | bytes 3145732

commit v2 on v0

v2 whole, which is shorter than its diff:
```python
import jax
import jax.numpy as jnp
from jax import lax
from jax.experimental import pallas as pl
from jax.experimental.pallas import tpu as pltpu
from jax.sharding import PartitionSpec as P

BLOCK = 128
REACH = 4
PIECES = 4
MESH = pl.DeviceIdType.MESH
EVERY, FRONT, HALVES = (0, 1, 2, 3), (0, 1), (0, 1)
COLUMN = [
    ("A1", "zp", None, EVERY), ("B1", "zo", None, EVERY), ("A2", "zo", "A1", EVERY), ("B2", "zp", "B1", EVERY),
    ("A3", "zp", "A2", FRONT), ("B3", "zo", "B2", FRONT), ("A4", "zo", "A3", FRONT), ("B4", "zp", "B3", FRONT),
    ("XO", "x", None, EVERY), ("XS", "w", None, HALVES), ("XA", "x", "A2", EVERY), ("XB", "x", "B2", EVERY),
    ("KA", "w", "XA", (0,)), ("KB", "w", "XB", (0,)), ("LA", "w", "KA", (0,)), ("LB", "w", "KB", (0,)),
    ("FA", "x", "A4", FRONT), ("FB", "x", "B4", FRONT),
]
ROW = [
    ("YF", "yf", None, HALVES), ("YN", "yn", None, HALVES), ("TF", "yf", "YF", HALVES), ("TN", "yn", "YN", HALVES),
    ("PF", "yf", "A1", HALVES), ("PN", "yn", "A1", HALVES), ("RF", "yf", "PF", (0,)), ("G", "zp", "TN", (1,)),
]
REVERSED = ("B1", "B2", "B3", "B4", "XB", "KB", "LB", "FB")
ROWS = tuple(n for n, k, d, s in ROW)
COARSE = ROWS + ("XS",)
LAST = ("TF", "TN", "PF", "PN", "RF", "G")


PRIO = {
    "A1": -6.5, "A2": 4.7, "A3": 7.6, "A4": -4.8, "B1": 6.7, "B2": 1.6, "B3": 0.1, "B4": -0.4,
    "FA": -0.8, "FB": -3.4, "G": 0.2, "KA": -3.4, "KB": 4.8, "LA": -7.8, "LB": -4.8, "PF": -5.0,
    "PN": -7.0, "RF": 6.5, "TF": 1.8, "TN": 3.4, "XA": 1.7, "XB": 1.3, "XO": -7.7, "XS": -5.5,
    "YF": -2.0, "YN": -1.3,
}


def plan(table):
    unit, lat = 5.24 / PIECES, 2.2
    dep = {n: d for n, k, d, s in table}
    link = {(n, i): "w" if (n, i) in (("XA", 0), ("XB", 0)) else k for n, k, d, s in table for i in s}
    dur = {n: unit * (2 if n in COARSE else 1) for n in dep}

    def needs(m):
        n, i = m
        if dep[n] is None:
            return []
        if n in ("PF", "PN"):
            return [("A1", 2 * i), ("A1", 2 * i + 1)]
        return [(dep[n], i)]

    todo = list(link)
    tail = {}
    for m in reversed(todo):
        tail[m] = dur[m[0]] + lat + max([tail[o] for o in tail if m in needs(o)], default=0.0)
    free = {k: 0.0 for k in link.values()}
    done, start, now = {}, {}, 0.0
    while todo:
        for k in free:
            ready = [m for m in todo if link[m] == k and all(done.get(o, 1e9) <= now + 1e-9 for o in needs(m))]
            if free[k] <= now + 1e-9 and ready:
                m = min(ready, key=lambda m: (PRIO[m[0]] - tail[m], m[1]))
                todo.remove(m)
                start[m] = now
                done[m] = now + dur[m[0]] + lat
                free[k] = now + dur[m[0]]
        if todo:
            now = min(t for t in list(free.values()) + list(done.values()) if t > now + 1e-9)
    events = [(t, 0, m) for m, t in start.items()]
    events += [(done[m] + 0.3, 1, m) for m in start if m[0] in LAST]
    return [(kind, m, needs(m)) for t, kind, m in sorted(events)]


def kernel(band_hbm, mat_hbm, sign_hbm, square_hbm, left, right, cube, relay, mask_ref, acc, mat_ref, square_ref, sign_ref, band_ref,
           left_recv, sib_recv, right_recv, cube_recv, relay_recv, send_sems, local_sems):
    r = lax.axis_index("row")
    c = lax.axis_index("col")
    l = lax.axis_index("layer")
    tile = mat_hbm.shape[0]
    width = tile // 2
    count = tile // BLOCK
    piece = tile // PIECES
    x, zh = r // 4, r % 4
    y, zl = c // 2, c % 2
    ol = 1 - zl
    f = 1 - 2 * zl
    order = (0, 3, 1, 2)

    band_copy = pltpu.make_async_copy(band_hbm, band_ref, local_sems.at[0])
    band_copy.start()
    mat_copies = {}
    for p in order:
        rows = pl.ds(p * piece, piece)
        mat_copies[p] = pltpu.make_async_copy(mat_hbm.at[rows], mat_ref.at[rows], local_sems.at[1 + p])
        mat_copies[p].start()

    def at(dx=0, dzh=0, dy=0, zlow=zl):
        return (((x + dx + 4) % 4) * 4 + (zh + dzh + 4) % 4, ((y + dy + 8) % 8) * 2 + zlow, l)

    sibling = (r, c, 1 - l)
    xup, xdown = at(dx=1), at(dx=-1)
    device = {"zp": at(zlow=ol), "zo": at(dzh=-f, zlow=ol), "x": xup, "w": xdown, "yf": at(dy=f), "yn": at(dy=-f)}

    barrier = pltpu.get_barrier_semaphore()
    for other in (sibling, *device.values()):
        pl.semaphore_signal(barrier, inc=1, device_id=other, device_id_type=MESH)

    column = 4 * c + lax.broadcasted_iota(jnp.int32, (1, tile), 1) // BLOCK
    own_left = 4 + zl
    own_right = 4 + zh
    mine = pl.ds(pl.multiple_of(l * width, width), width)
    band_copy.wait()

    def own_piece(a):
        hit = column == band_ref[0, count * r + a]
        for j in range(1, band_ref.shape[0]):
            hit = hit | (column == band_ref[j, count * r + a])
        row_mask = jnp.where(hit, 1.0, 0.0).astype(jnp.float32)
        mask_ref[pl.ds(a, 1), :] = row_mask
        rows = pl.ds(a * BLOCK, BLOCK)
        mat_copies[a].wait()
        low = (mat_ref[rows, :] * row_mask).astype(jnp.bfloat16)
        left[own_left, 0, rows, :] = low[:, :width]
        left[own_left, 1, rows, :] = low[:, width:]
        right[own_right, rows, :] = left[own_left, l, rows, :]

    sent = []

    def remote(src, dst, recv_sem, target):
        return pltpu.make_async_remote_copy(
            src_ref=src, dst_ref=dst, send_sem=send_sems.at[len(sent)], recv_sem=recv_sem,
            device_id=target, device_id_type=MESH)

    def send(src, dst, recv_sem, target):
        copy = remote(src, dst, recv_sem, target)
        copy.start()
        sent.append((copy, None))

    def left_device(copies):
        for copy, only in copies:
            if only is None:
                copy.wait_send()
            else:
                pl.when(only)(copy.wait_send)

    def arrival(ref, sem):
        return pltpu.make_async_remote_copy(
            src_ref=ref, dst_ref=ref, send_sem=send_sems.at[0], recv_sem=sem,
            device_id=sibling, device_id_type=MESH)

    def arrived(ref, sem):
        arrival(ref, sem).wait_recv()

    links = {n: k for n, k, d, s in COLUMN + ROW}
    left_slot = {"YF": 4 - 2 * f + zl, "YN": 4 + 2 * f + zl, "TF": 4 - 4 * f + zl, "TN": 4 + 4 * f + zl,
                 "PF": 4 - 2 * f + ol, "PN": 4 + 2 * f + ol, "RF": 4 - 4 * f + ol, "G": 4 - 4 * f + ol, "A1": 4 + ol}
    near_a, near_b, far = (zh - f + 4) % 4, (zh + f + 4) % 4, (zh + 2) % 4
    halves = [pl.ds(j * width, width) for j in range(2)]
    edge = (zh == 0) | (zh == 3)
    side = (jnp.where(zh < 2, xdown[0], xup[0]), c, l)

    def gather(buf, sem, square, make_piece):
        phase = 0 if square else 1
        waited, made = set(), set()

        def rows_of(name, i):
            if name in COARSE:
                return halves[i]
            p = PIECES - 1 - i if name in REVERSED else i
            return pl.ds(p * piece, piece)

        def ensure(name, i):
            for p in ((2 * i, 2 * i + 1) if name in COARSE else (PIECES - 1 - i if name in REVERSED else i,)):
                if p not in made:
                    made.add(p)
                    make_piece(p)
                    if len(made) == 1 and square:
                        pl.semaphore_wait(barrier, 7)

        def landing(name, i):
            if name in left_slot and (square or name != "A1"):
                slot = left_slot[name]
                return left.at[slot, l, rows_of(name, i)], left_recv.at[slot, i]
            if name in ("XA", "XB", "KA", "KB"):
                slot = 12 if name in ("XA", "XB") else 13
                return buf.at[slot, rows_of(name, i)], sem.at[slot, 0 if name in ("XA", "KA") else 1]
            if name in ("A1", "B1", "A3", "B3"):
                place = {"A1": 0, "B1": PIECES, "A3": 2 * PIECES, "B3": 2 * PIECES + 2}[name] + i
                return relay.at[phase, place], relay_recv.at[phase, place]
            slot = 4 + {"A2": near_a, "B2": near_b, "A4": far, "B4": far}[name]
            return buf.at[slot, rows_of(name, i)], sem.at[slot, i + (2 if name == "B4" else 0)]

        def wait(name, i):
            if (name, i) in waited:
                return
            waited.add((name, i))
            arrived(*landing(name, i))
            if name in left_slot and square:
                if name == "A1":
                    if (name, i ^ 1) not in waited:
                        return
                    i = i // 2
                ref = left.at[left_slot[name], l, halves[i]]
                send(ref, ref, sib_recv.at[left_slot[name], i], sibling)

        def away(name, i):
            if name in ("XO", "XS", "XA", "XB", "LA", "LB", "FA", "FB"):
                zs = {"A": near_a, "B": near_b}.get(name[1], zh) if name[0] != "F" else far
                higher = {"XO": zh < 2, "XS": zh >= 2}.get(name, zs > zh)
                slot = jnp.where(higher, zs, 8 + zs)
                target = jnp.where(higher, xup[0], xdown[0])
                index = i + (2 if name == "FB" else 0)
                if name in ("LA", "LB"):
                    target = side[0]
                if name in ("XA", "XB") and i == 0:
                    slot = jnp.where(edge, 12, slot)
                    target = jnp.where(edge, side[0], target)
                    index = jnp.where(edge, 0 if name == "XA" else 1, 0)
                return buf.at[slot, rows_of(name, i)], sem.at[slot, index], (target, c, l)
            if name in ("KA", "KB"):
                return *landing(name, i), side
            target = device[links[name]]
            if name == "A1" and square:
                return left.at[own_left, l, rows_of(name, i)], left_recv.at[own_left, i], target
            if name == "G":
                slot = left_slot["TN"]
                return left.at[slot, l, halves[i]], left_recv.at[slot, i], target
            if name in ("A1", "B1", "A3", "B3") or name in ROWS:
                return *landing(name, i), target
            slot = 4 + {"A2": zh, "B2": near_a, "A4": near_b, "B4": far}[name]
            return buf.at[slot, rows_of(name, i)], sem.at[slot, i + (2 if name == "B4" else 0)], target

        for kind, (name, i), needs in plan(COLUMN + ROW if square else COLUMN):
            if kind == 1:
                wait(name, i)
            elif name in ("KA", "KB", "LA", "LB"):
                source, recv = landing(*needs[0])
                before = arrival(source, recv)
                copy = remote(source, *away(name, i))
                sent.append((copy, edge))

                @pl.when(edge)
                def _():
                    before.wait_recv()
                    copy.start()
            else:
                for m in needs:
                    wait(*m)
                if name in ROWS and needs:
                    source = left.at[left_slot[needs[0][0]], l, halves[i]]
                elif needs:
                    source = landing(*needs[0])[0]
                else:
                    ensure(name, i)
                    source = left.at[own_left, l, halves[i]] if name in ROWS else buf.at[own_right, rows_of(name, i)]
                send(source, *away(name, i))

    def gather_end(buf, sem):
        for i in range(PIECES):
            slot = jnp.where(zh < 2, zh, 8 + zh)
            arrived(buf.at[slot, pl.ds(i * piece, piece)], sem.at[slot, i])
        for i in range(2):
            slot = jnp.where(zh < 2, 8 + zh, zh)
            arrived(buf.at[slot, halves[i]], sem.at[slot, i])
        slot = jnp.where(far > zh, far, 8 + far)
        for i in range(2):
            arrived(buf.at[slot, pl.ds(i * piece, piece)], sem.at[slot, i])
            arrived(buf.at[slot, pl.ds((PIECES - 1 - i) * piece, piece)], sem.at[slot, i + 2])
        for i in range(PIECES):
            for p, zs in ((i, near_a), (PIECES - 1 - i, near_b)):
                slot = jnp.where(zs > zh, zs, 8 + zs)
                arrived(buf.at[slot, pl.ds(p * piece, piece)], sem.at[slot, i])

    first = jnp.maximum(jnp.maximum(r, c) - REACH, 0)
    stop = jnp.minimum(jnp.minimum(r, c) + REACH, 15) + 1
    inside = (c - r <= REACH) & (r - c <= REACH)
    stop = jnp.where(inside, stop, first)
    plane = 4 * x

    def product(buf, rows, chosen):
        def body(k, carry):
            @pl.when(chosen(k))
            def _():
                ls = k - c + zl + 4
                rs = k - r + zh + 4
                acc[rows, :] += jnp.dot(
                    left[ls, 0, rows, :], buf[rs, :width, :], preferred_element_type=jnp.float32) + jnp.dot(
                    left[ls, 1, rows, :], buf[rs, width:, :], preferred_element_type=jnp.float32)
            return carry

        lax.fori_loop(first, stop, body, 0)

    def in_plane(k):
        return (k >= plane) & (k < plane + 4)

    def early_left(k):
        return in_plane(k) & (k != c - 3 * f) & (k != c - 4 * f)

    def later(chosen):
        return lambda k: jnp.logical_not(chosen(k))

    def square_piece(a):
        rows = pl.ds(a * BLOCK, BLOCK)
        product(right, rows, later(early_left))
        value = acc[rows, :] * mask_ref[pl.ds(a, 1), mine]
        square_ref[rows, :] = value
        cube[own_right, rows, :] = value.astype(jnp.bfloat16)
        acc[rows, :] = jnp.zeros((BLOCK, width), jnp.float32)

    gather(right, right_recv, True, own_piece)
    acc[...] = jnp.zeros_like(acc)

    def from_sibling(names):
        for name in names:
            for j in ((0, 1) if name != "RF" else (0,)) if name != "G" else (1,):
                arrived(left.at[left_slot[name], 1 - l, halves[j]], sib_recv.at[left_slot[name], j])

    from_sibling(("A1", "YF", "YN", "PF", "PN", "TN"))
    for rows in halves:
        product(right, rows, early_left)
    from_sibling(("TF", "RF", "G"))
    gather_end(right, right_recv)

    early = len(sent)
    gather(cube, cube_recv, False, square_piece)
    square_copy = pltpu.make_async_copy(square_ref, square_hbm, local_sems.at[0])
    square_copy.start()
    left_device(sent[:early])
    for rows in halves:
        product(cube, rows, in_plane)
    gather_end(cube, cube_recv)
    sign_copies = []
    for j, rows in enumerate(halves):
        product(cube, rows, later(in_plane))
        for a in range(j * count // 2, (j + 1) * count // 2):
            block = pl.ds(a * BLOCK, BLOCK)
            row_mask = mask_ref[pl.ds(a, 1), mine]
            sparse = mat_ref[block, mine] * row_mask
            sign_ref[block, :] = row_mask * (1.5 * sparse - 0.5 * acc[block, :])
        sign_copies.append(pltpu.make_async_copy(sign_ref.at[rows], sign_hbm.at[rows], local_sems.at[1 + j]))
        sign_copies[-1].start()

    left_device(sent[early:])
    square_copy.wait()
    for copy in sign_copies:
        copy.wait()


def per_device(matrix, band_cols):
    tile = matrix.shape[0]
    width = tile // 2
    piece = tile // PIECES
    out = jax.ShapeDtypeStruct((tile, width), jnp.float32)
    return pl.pallas_call(
        kernel,
        out_shape=(out, out),
        in_specs=[pl.BlockSpec(memory_space=pltpu.HBM)] * 2,
        out_specs=(pl.BlockSpec(memory_space=pltpu.HBM),) * 2,
        scratch_shapes=[
            pltpu.VMEM((10, 2, tile, width), jnp.bfloat16),
            pltpu.VMEM((14, tile, width), jnp.bfloat16),
            pltpu.VMEM((14, tile, width), jnp.bfloat16),
            pltpu.VMEM((2, 3 * PIECES, piece, width), jnp.bfloat16),
            pltpu.VMEM((8, tile), jnp.float32),
            pltpu.VMEM((tile, width), jnp.float32),
            pltpu.VMEM((tile, tile), jnp.float32),
            pltpu.VMEM((tile, width), jnp.float32),
            pltpu.VMEM((tile, width), jnp.float32),
            pltpu.SMEM(band_cols.shape[::-1], jnp.int32),
            pltpu.SemaphoreType.DMA((10, PIECES)),
            pltpu.SemaphoreType.DMA((10, 2)),
            pltpu.SemaphoreType.DMA((14, PIECES)),
            pltpu.SemaphoreType.DMA((14, PIECES)),
            pltpu.SemaphoreType.DMA((2, 3 * PIECES)),
            pltpu.SemaphoreType.DMA((128,)),
            pltpu.SemaphoreType.DMA((1 + PIECES,)),
        ],
        compiler_params=pltpu.CompilerParams(
            collective_id=0, has_side_effects=True, vmem_limit_bytes=48 * 2**20),
        cost_estimate=pl.CostEstimate(flops=4 * 10**9, bytes_accessed=2 * 2**20, transcendentals=0),
    )(band_cols.T, matrix)


def solution(mesh):
    in_specs = (P("row", "col"), P())
    out_specs = (P("row", ("col", "layer")), P("row", ("col", "layer")))
    return jax.shard_map(
        per_device, mesh=mesh, in_specs=in_specs, out_specs=out_specs, check_vma=False
    )
```

time: 734 us -> 72.7 us (0.10)
  the two profiles are of different devices: /device:TPU:1 before, /device:TPU:26 now
where the time goes in v2:
time: 72.7 us; the launch traced here: 72.5 us
  Pallas kernels  68.4 us (94%)
  local copies, waits for them, and re-layouts  3.51 us (5%)
    pallas_call x1, Pallas kernels, per_device(): pl.pallas_call(kernel, out_shape=(out, out), in_specs=[pl.BlockSpec(memor...  68.4 us
    unnamed x6, local copies, waits for them, and re-layouts  3.51 us

profile of v2, /device:TPU:26, one launch (start us, length us, event | category | flops | bytes accessed | tf_op | source)
XLA Modules:
  0.0 72.5 jit_solution(15156054957664552674)
XLA Ops:
  0.6 0.0 copy-start
  0.6 1.2 %copy-done = f32[512,512]{1,0:T(8,128)S(1)} copy-done((f32[512,512]{1,0:T(8,128)S(1)}, f32[512,512]{1,0:T(8,128)}, u32[]{:S(2)}) %copy-start) | copy-done | bytes 1048600
  1.9 0.0 copy-start.1
  1.9 0.7 copy-done.1
  2.6 68.4 %shard_map.41 = (f32[512,256]{1,0:T(8,128)S(1)}, f32[512,256]{1,0:T(8,128)S(1)}) custom-call(s32[17,64]{1,0:T(8,128)S(1)} %bitcast.1, f32[512,512]{1,0:T(8,128)S(1)} %copy-done), custom_call_target="tpu_custom_call" | custom-call | flops 4000000000 | bytes 2097152 | tf_op jit(solution)/shard_map/pallas_call | solution.py:354
  70.9 0.8 %copy.6 = f32[512,256]{1,0:T(8,128)} copy(f32[512,256]{1,0:T(8,128)S(1)} %get-tuple-element.4) | data formatting | bytes 1048576
  71.7 0.8 %copy.7 = f32[512,256]{1,0:T(8,128)} copy(f32[512,256]{1,0:T(8,128)S(1)} %get-tuple-element.5) | data formatting | bytes 1048576
Async XLA Ops:
  0.6 1.2 %copy-start = (f32[512,512]{1,0:T(8,128)S(1)}, f32[512,512]{1,0:T(8,128)}, u32[]{:S(2)}) copy-start(f32[512,512]{1,0:T(8,128)} %mat_hbm.1) | copy-start | bytes 3145732
  1.9 0.7 copy-start.1

commit v3 on v2

--- a/solution.py
+++ b/solution.py
@@ -9,66 +9,26 @@
 REACH = 4
 PIECES = 4
 MESH = pl.DeviceIdType.MESH
-EVERY, FRONT, HALVES = (0, 1, 2, 3), (0, 1), (0, 1)
-COLUMN = [
-    ("A1", "zp", None, EVERY), ("B1", "zo", None, EVERY), ("A2", "zo", "A1", EVERY), ("B2", "zp", "B1", EVERY),
-    ("A3", "zp", "A2", FRONT), ("B3", "zo", "B2", FRONT), ("A4", "zo", "A3", FRONT), ("B4", "zp", "B3", FRONT),
-    ("XO", "x", None, EVERY), ("XS", "w", None, HALVES), ("XA", "x", "A2", EVERY), ("XB", "x", "B2", EVERY),
-    ("KA", "w", "XA", (0,)), ("KB", "w", "XB", (0,)), ("LA", "w", "KA", (0,)), ("LB", "w", "KB", (0,)),
-    ("FA", "x", "A4", FRONT), ("FB", "x", "B4", FRONT),
-]
-ROW = [
-    ("YF", "yf", None, HALVES), ("YN", "yn", None, HALVES), ("TF", "yf", "YF", HALVES), ("TN", "yn", "YN", HALVES),
-    ("PF", "yf", "A1", HALVES), ("PN", "yn", "A1", HALVES), ("RF", "yf", "PF", (0,)), ("G", "zp", "TN", (1,)),
-]
+NEEDS = {"A2": "A1", "B2": "B1", "A3": "A2", "B3": "B2", "A4": "A3", "B4": "B3", "XA": "A2", "XB": "B2", "KA": "XA", "KB": "XB",
+         "LA": "KA", "LB": "KB", "FA": "A4", "FB": "B4", "TF": "YF", "TN": "YN", "PF": "A1", "PN": "A1", "RF": "PF", "G": "TN"}
+LINKS = {"A1": "zp", "B1": "zo", "A2": "zo", "B2": "zp", "A3": "zp", "B3": "zo", "A4": "zo", "B4": "zp", "YF": "yf", "YN": "yn",
+         "TF": "yf", "TN": "yn", "PF": "yf", "PN": "yn", "RF": "yf", "G": "zp"}
 REVERSED = ("B1", "B2", "B3", "B4", "XB", "KB", "LB", "FB")
-ROWS = tuple(n for n, k, d, s in ROW)
+ROWS = ("YF", "YN", "TF", "TN", "PF", "PN", "RF", "G")
 COARSE = ROWS + ("XS",)
-LAST = ("TF", "TN", "PF", "PN", "RF", "G")
-
-
-PRIO = {
-    "A1": -6.5, "A2": 4.7, "A3": 7.6, "A4": -4.8, "B1": 6.7, "B2": 1.6, "B3": 0.1, "B4": -0.4,
-    "FA": -0.8, "FB": -3.4, "G": 0.2, "KA": -3.4, "KB": 4.8, "LA": -7.8, "LB": -4.8, "PF": -5.0,
-    "PN": -7.0, "RF": 6.5, "TF": 1.8, "TN": 3.4, "XA": 1.7, "XB": 1.3, "XO": -7.7, "XS": -5.5,
-    "YF": -2.0, "YN": -1.3,
-}
-
-
-def plan(table):
-    unit, lat = 5.24 / PIECES, 2.2
-    dep = {n: d for n, k, d, s in table}
-    link = {(n, i): "w" if (n, i) in (("XA", 0), ("XB", 0)) else k for n, k, d, s in table for i in s}
-    dur = {n: unit * (2 if n in COARSE else 1) for n in dep}
-
-    def needs(m):
-        n, i = m
-        if dep[n] is None:
-            return []
-        if n in ("PF", "PN"):
-            return [("A1", 2 * i), ("A1", 2 * i + 1)]
-        return [(dep[n], i)]
-
-    todo = list(link)
-    tail = {}
-    for m in reversed(todo):
-        tail[m] = dur[m[0]] + lat + max([tail[o] for o in tail if m in needs(o)], default=0.0)
-    free = {k: 0.0 for k in link.values()}
-    done, start, now = {}, {}, 0.0
-    while todo:
-        for k in free:
-            ready = [m for m in todo if link[m] == k and all(done.get(o, 1e9) <= now + 1e-9 for o in needs(m))]
-            if free[k] <= now + 1e-9 and ready:
-                m = min(ready, key=lambda m: (PRIO[m[0]] - tail[m], m[1]))
-                todo.remove(m)
-                start[m] = now
-                done[m] = now + dur[m[0]] + lat
-                free[k] = now + dur[m[0]]
-        if todo:
-            now = min(t for t in list(free.values()) + list(done.values()) if t > now + 1e-9)
-    events = [(t, 0, m) for m, t in start.items()]
-    events += [(done[m] + 0.3, 1, m) for m in start if m[0] in LAST]
-    return [(kind, m, needs(m)) for t, kind, m in sorted(events)]
+SQUARE_ORDER = (
+    "A10", "B13", "YF0", "A11", "B11", "YF1", "XO0", "B10", "A13", "XO3", "YN1", "A20", "A12", "YN0",
+    "B12", "B21", "A21", "XS1", "TF0", "XO2", "B20", "PF0", "B23", "TN1", "XO1", "A22", "XA0", "A23",
+    "A30", "XB1", "PN0", "B31", "TF1", "XA1", "A31", "XB0", "PF1", "B30", "PN1", "B22", "XB3", "XS0",
+    "XA2", "KA0", "A40", "XA3", "A41", "B41", "TN0", "?TF0", "RF0", "KB0", "XB2", "B40", "G1", "?TF1",
+    "FA0", "?PN1", "FA1", "LA0", "?PF0", "FB1", "?TN0", "LB0", "?PF1", "?TN1", "FB0", "?G1", "?RF0", "?PN0",
+)
+CUBE_ORDER = (
+    "A10", "B10", "XO0", "XS0", "A11", "B11", "XO1", "A12", "B12", "XO2", "XS1", "A13", "A20", "XO3",
+    "A21", "B20", "B13", "B21", "XA0", "A22", "B22", "XA1", "XB0", "A30", "B30", "XB1", "B23", "B31",
+    "KA0", "XB2", "A23", "A31", "KB0", "XA2", "A40", "B40", "XB3", "B41", "LA0", "A41", "XA3", "LB0",
+    "FB0", "FB1", "FA0", "FA1",
+)
 
 
 def kernel(band_hbm, mat_hbm, sign_hbm, square_hbm, left, right, cube, relay, mask_ref, acc, mat_ref, square_ref, sign_ref, band_ref,
@@ -151,7 +111,6 @@
     def arrived(ref, sem):
         arrival(ref, sem).wait_recv()
 
-    links = {n: k for n, k, d, s in COLUMN + ROW}
     left_slot = {"YF": 4 - 2 * f + zl, "YN": 4 + 2 * f + zl, "TF": 4 - 4 * f + zl, "TN": 4 + 4 * f + zl,
                  "PF": 4 - 2 * f + ol, "PN": 4 + 2 * f + ol, "RF": 4 - 4 * f + ol, "G": 4 - 4 * f + ol, "A1": 4 + ol}
     near_a, near_b, far = (zh - f + 4) % 4, (zh + f + 4) % 4, (zh + 2) % 4
@@ -175,7 +134,7 @@
                     made.add(p)
                     make_piece(p)
                     if len(made) == 1 and square:
-                        pl.semaphore_wait(barrier, 7)
+                        pl.semaphore_wait(barrier, 1 + len(device))
 
         def landing(name, i):
             if name in left_slot and (square or name != "A1"):
@@ -219,7 +178,7 @@
                 return buf.at[slot, rows_of(name, i)], sem.at[slot, index], (target, c, l)
             if name in ("KA", "KB"):
                 return *landing(name, i), side
-            target = device[links[name]]
+            target = device[LINKS[name]]
             if name == "A1" and square:
                 return left.at[own_left, l, rows_of(name, i)], left_recv.at[own_left, i], target
             if name == "G":
@@ -230,8 +189,12 @@
             slot = 4 + {"A2": zh, "B2": near_a, "A4": near_b, "B4": far}[name]
             return buf.at[slot, rows_of(name, i)], sem.at[slot, i + (2 if name == "B4" else 0)], target
 
-        for kind, (name, i), needs in plan(COLUMN + ROW if square else COLUMN):
-            if kind == 1:
+        for token in SQUARE_ORDER if square else CUBE_ORDER:
+            name, i = token[:-1].lstrip("?"), int(token[-1])
+            needs = [(NEEDS[name], i)] if NEEDS.get(name) else []
+            if name in ("PF", "PN"):
+                needs = [("A1", 2 * i), ("A1", 2 * i + 1)]
+            if token[0] == "?":
                 wait(name, i)
             elif name in ("KA", "KB", "LA", "LB"):
                 source, recv = landing(*needs[0])
@@ -255,21 +218,25 @@
                     source = left.at[own_left, l, halves[i]] if name in ROWS else buf.at[own_right, rows_of(name, i)]
                 send(source, *away(name, i))
 
-    def gather_end(buf, sem):
+    def own_arrived(buf, sem):
         for i in range(PIECES):
             slot = jnp.where(zh < 2, zh, 8 + zh)
             arrived(buf.at[slot, pl.ds(i * piece, piece)], sem.at[slot, i])
         for i in range(2):
             slot = jnp.where(zh < 2, 8 + zh, zh)
             arrived(buf.at[slot, halves[i]], sem.at[slot, i])
+
+    def near_arrived(buf, sem):
+        for i in range(PIECES):
+            for p, zs in ((i, near_a), (PIECES - 1 - i, near_b)):
+                slot = jnp.where(zs > zh, zs, 8 + zs)
+                arrived(buf.at[slot, pl.ds(p * piece, piece)], sem.at[slot, i])
+
+    def far_arrived(buf, sem):
         slot = jnp.where(far > zh, far, 8 + far)
         for i in range(2):
             arrived(buf.at[slot, pl.ds(i * piece, piece)], sem.at[slot, i])
             arrived(buf.at[slot, pl.ds((PIECES - 1 - i) * piece, piece)], sem.at[slot, i + 2])
-        for i in range(PIECES):
-            for p, zs in ((i, near_a), (PIECES - 1 - i, near_b)):
-                slot = jnp.where(zs > zh, zs, 8 + zs)
-                arrived(buf.at[slot, pl.ds(p * piece, piece)], sem.at[slot, i])
 
     first = jnp.maximum(jnp.maximum(r, c) - REACH, 0)
     stop = jnp.minimum(jnp.minimum(r, c) + REACH, 15) + 1
@@ -290,18 +257,23 @@
 
         lax.fori_loop(first, stop, body, 0)
 
-    def in_plane(k):
-        return (k >= plane) & (k < plane + 4)
-
-    def early_left(k):
-        return in_plane(k) & (k != c - 3 * f) & (k != c - 4 * f)
-
-    def later(chosen):
-        return lambda k: jnp.logical_not(chosen(k))
+    far_k = jnp.where(far > zh, plane - 4 + far, plane + 4 + far)
+
+    def early(k):
+        return ((k >= plane) & (k < plane + 4)) | (k == r - 4) | (k == r + 4)
+
+    def early_both(k):
+        return early(k) & (k != c + 3 * f) & (k != c - 3 * f)
+
+    def is_far(k):
+        return k == far_k
+
+    def middle(chosen):
+        return lambda k: jnp.logical_not(chosen(k) | is_far(k))
 
     def square_piece(a):
         rows = pl.ds(a * BLOCK, BLOCK)
-        product(right, rows, later(early_left))
+        product(right, rows, is_far)
         value = acc[rows, :] * mask_ref[pl.ds(a, 1), mine]
         square_ref[rows, :] = value
         cube[own_right, rows, :] = value.astype(jnp.bfloat16)
@@ -315,23 +287,31 @@
             for j in ((0, 1) if name != "RF" else (0,)) if name != "G" else (1,):
                 arrived(left.at[left_slot[name], 1 - l, halves[j]], sib_recv.at[left_slot[name], j])
 
-    from_sibling(("A1", "YF", "YN", "PF", "PN", "TN"))
+    from_sibling(("A1", "YF", "YN", "PF", "TF", "TN"))
+    own_arrived(right, right_recv)
     for rows in halves:
-        product(right, rows, early_left)
-    from_sibling(("TF", "RF", "G"))
-    gather_end(right, right_recv)
-
-    early = len(sent)
+        product(right, rows, early_both)
+    from_sibling(("PN", "RF", "G"))
+    near_arrived(right, right_recv)
+    for rows in halves:
+        product(right, rows, middle(early_both))
+    far_arrived(right, right_recv)
+
+    started = len(sent)
     gather(cube, cube_recv, False, square_piece)
     square_copy = pltpu.make_async_copy(square_ref, square_hbm, local_sems.at[0])
     square_copy.start()
-    left_device(sent[:early])
+    left_device(sent[:started])
+    own_arrived(cube, cube_recv)
     for rows in halves:
-        product(cube, rows, in_plane)
-    gather_end(cube, cube_recv)
+        product(cube, rows, early)
+    near_arrived(cube, cube_recv)
+    for rows in halves:
+        product(cube, rows, middle(early))
+    far_arrived(cube, cube_recv)
     sign_copies = []
     for j, rows in enumerate(halves):
-        product(cube, rows, later(in_plane))
+        product(cube, rows, is_far)
         for a in range(j * count // 2, (j + 1) * count // 2):
             block = pl.ds(a * BLOCK, BLOCK)
             row_mask = mask_ref[pl.ds(a, 1), mine]
@@ -340,7 +320,7 @@
         sign_copies.append(pltpu.make_async_copy(sign_ref.at[rows], sign_hbm.at[rows], local_sems.at[1 + j]))
         sign_copies[-1].start()
 
-    left_device(sent[early:])
+    left_device(sent[started:])
     square_copy.wait()
     for copy in sign_copies:
         copy.wait()
@@ -376,7 +356,7 @@
             pltpu.SemaphoreType.DMA((1 + PIECES,)),
         ],
         compiler_params=pltpu.CompilerParams(
-            collective_id=0, has_side_effects=True, vmem_limit_bytes=48 * 2**20),
+            collective_id=0, has_side_effects=True, vmem_limit_bytes=105 * 2**19),
         cost_estimate=pl.CostEstimate(flops=4 * 10**9, bytes_accessed=2 * 2**20, transcendentals=0),
     )(band_cols.T, matrix)
 

time: 72.7 us -> 69.6 us (0.957)
  the two profiles are of different devices: /device:TPU:26 before, /device:TPU:1 now
where the time goes in v3:
time: 69.6 us; the launch traced here: 68.2 us
  Pallas kernels  65.3 us (94%)
  local copies, waits for them, and re-layouts  2.29 us (3%)
    pallas_call x1, Pallas kernels, per_device(): pl.pallas_call(kernel, out_shape=(out, out), in_specs=[pl.BlockSpec(memor...  65.3 us
    unnamed x4, local copies, waits for them, and re-layouts  2.29 us

profile of v3, /device:TPU:1, one launch (start us, length us, event | category | flops | bytes accessed | tf_op | source)
XLA Modules:
  0.0 68.2 jit_solution(15656424999162352142)
XLA Ops:
  0.6 0.0 copy-start
  0.6 0.7 %copy-done = s32[64,17]{0,1:T(8,128)S(1)} copy-done((s32[64,17]{0,1:T(8,128)S(1)}, s32[64,17]{0,1:T(8,128)}, u32[]{:S(2)}) %copy-start) | copy-done | bytes 4376
  1.3 65.3 %shard_map.41 = (f32[512,256]{1,0:T(8,128)S(1)}, f32[512,256]{1,0:T(8,128)S(1)}) custom-call(s32[17,64]{1,0:T(8,128)S(1)} %bitcast.1, f32[512,512]{1,0:T(8,128)} %mat_hbm.1), custom_call_target="tpu_custom_call" | custom-call | flops 4000000000 | bytes 2097152 | tf_op jit(solution)/shard_map/pallas_call | solution.py:334
  66.6 0.8 %copy.6 = f32[512,256]{1,0:T(8,128)} copy(f32[512,256]{1,0:T(8,128)S(1)} %get-tuple-element.4) | data formatting | bytes 1048576
  67.4 0.8 %copy.7 = f32[512,256]{1,0:T(8,128)} copy(f32[512,256]{1,0:T(8,128)S(1)} %get-tuple-element.5) | data formatting | bytes 1048576
Async XLA Ops:
  0.6 0.7 %copy-start = (s32[64,17]{0,1:T(8,128)S(1)}, s32[64,17]{0,1:T(8,128)}, u32[]{:S(2)}) copy-start(s32[64,17]{0,1:T(8,128)} %param.3) | copy-start | bytes 13060

commit v4 on v3

--- a/solution.py
+++ b/solution.py
@@ -244,18 +244,22 @@
     stop = jnp.where(inside, stop, first)
     plane = 4 * x
 
+    def add_product(buf, rows, k):
+        ls = k - c + zl + 4
+        rs = k - r + zh + 4
+        acc[rows, :] += jnp.dot(
+            left[ls, 0, rows, :], buf[rs, :width, :], preferred_element_type=jnp.float32) + jnp.dot(
+            left[ls, 1, rows, :], buf[rs, width:, :], preferred_element_type=jnp.float32)
+
     def product(buf, rows, chosen):
         def body(k, carry):
-            @pl.when(chosen(k))
-            def _():
-                ls = k - c + zl + 4
-                rs = k - r + zh + 4
-                acc[rows, :] += jnp.dot(
-                    left[ls, 0, rows, :], buf[rs, :width, :], preferred_element_type=jnp.float32) + jnp.dot(
-                    left[ls, 1, rows, :], buf[rs, width:, :], preferred_element_type=jnp.float32)
+            pl.when(chosen(k))(lambda: add_product(buf, rows, k))
             return carry
 
         lax.fori_loop(first, stop, body, 0)
+
+    def far_product(buf, rows):
+        pl.when((far_k >= first) & (far_k < stop))(lambda: add_product(buf, rows, far_k))
 
     far_k = jnp.where(far > zh, plane - 4 + far, plane + 4 + far)
 
@@ -265,15 +269,12 @@
     def early_both(k):
         return early(k) & (k != c + 3 * f) & (k != c - 3 * f)
 
-    def is_far(k):
-        return k == far_k
-
     def middle(chosen):
-        return lambda k: jnp.logical_not(chosen(k) | is_far(k))
+        return lambda k: jnp.logical_not(chosen(k) | (k == far_k))
 
     def square_piece(a):
         rows = pl.ds(a * BLOCK, BLOCK)
-        product(right, rows, is_far)
+        far_product(right, rows)
         value = acc[rows, :] * mask_ref[pl.ds(a, 1), mine]
         square_ref[rows, :] = value
         cube[own_right, rows, :] = value.astype(jnp.bfloat16)
@@ -308,10 +309,11 @@
     near_arrived(cube, cube_recv)
     for rows in halves:
         product(cube, rows, middle(early))
+    left_device(sent[started:])
     far_arrived(cube, cube_recv)
     sign_copies = []
     for j, rows in enumerate(halves):
-        product(cube, rows, is_far)
+        far_product(cube, rows)
         for a in range(j * count // 2, (j + 1) * count // 2):
             block = pl.ds(a * BLOCK, BLOCK)
             row_mask = mask_ref[pl.ds(a, 1), mine]
@@ -320,7 +322,6 @@
         sign_copies.append(pltpu.make_async_copy(sign_ref.at[rows], sign_hbm.at[rows], local_sems.at[1 + j]))
         sign_copies[-1].start()
 
-    left_device(sent[started:])
     square_copy.wait()
     for copy in sign_copies:
         copy.wait()

time: 69.6 us -> 68.9 us (0.990)
  no operation moved by 1% of the time
where the time goes in v4:
time: 68.9 us; the launch traced here: 68.1 us
  Pallas kernels  65.2 us (95%)
  local copies, waits for them, and re-layouts  2.29 us (3%)
    pallas_call x1, Pallas kernels, per_device(): pl.pallas_call(kernel, out_shape=(out, out), in_specs=[pl.BlockSpec(memor...  65.2 us
    unnamed x4, local copies, waits for them, and re-layouts  2.29 us

profile of v4, /device:TPU:1, one launch (start us, length us, event | category | flops | bytes accessed | tf_op | source)
XLA Modules:
  0.0 68.1 jit_solution(17750196517546517109)
XLA Ops:
  0.6 0.0 copy-start
  0.6 0.7 %copy-done = s32[64,17]{0,1:T(8,128)S(1)} copy-done((s32[64,17]{0,1:T(8,128)S(1)}, s32[64,17]{0,1:T(8,128)}, u32[]{:S(2)}) %copy-start) | copy-done | bytes 4376
  1.3 65.2 %shard_map.41 = (f32[512,256]{1,0:T(8,128)S(1)}, f32[512,256]{1,0:T(8,128)S(1)}) custom-call(s32[17,64]{1,0:T(8,128)S(1)} %bitcast.1, f32[512,512]{1,0:T(8,128)} %mat_hbm.1), custom_call_target="tpu_custom_call" | custom-call | flops 4000000000 | bytes 2097152 | tf_op jit(solution)/shard_map/pallas_call | solution.py:335
  66.5 0.8 %copy.6 = f32[512,256]{1,0:T(8,128)} copy(f32[512,256]{1,0:T(8,128)S(1)} %get-tuple-element.4) | data formatting | bytes 1048576
  67.3 0.8 %copy.7 = f32[512,256]{1,0:T(8,128)} copy(f32[512,256]{1,0:T(8,128)S(1)} %get-tuple-element.5) | data formatting | bytes 1048576
Async XLA Ops:
  0.6 0.7 %copy-start = (s32[64,17]{0,1:T(8,128)S(1)}, s32[64,17]{0,1:T(8,128)}, u32[]{:S(2)}) copy-start(s32[64,17]{0,1:T(8,128)} %param.3) | copy-start | bytes 13060

commit v5 on v4

--- a/solution.py
+++ b/solution.py
@@ -44,26 +44,25 @@
     y, zl = c // 2, c % 2
     ol = 1 - zl
     f = 1 - 2 * zl
-    order = (0, 3, 1, 2)
+
+    def at(dx=0, dzh=0, dy=0, zlow=zl):
+        return (((x + dx + 4) % 4) * 4 + (zh + dzh + 4) % 4, ((y + dy + 8) % 8) * 2 + zlow, l)
+
+    sibling = (r, c, 1 - l)
+    xup, xdown = at(dx=1), at(dx=-1)
+    device = {"zp": at(zlow=ol), "zo": at(dzh=-f, zlow=ol), "x": xup, "w": xdown, "yf": at(dy=f), "yn": at(dy=-f)}
+
+    barrier = pltpu.get_barrier_semaphore()
+    for other in (sibling, *device.values()):
+        pl.semaphore_signal(barrier, inc=1, device_id=other, device_id_type=MESH)
 
     band_copy = pltpu.make_async_copy(band_hbm, band_ref, local_sems.at[0])
     band_copy.start()
     mat_copies = {}
-    for p in order:
+    for p in range(PIECES):
         rows = pl.ds(p * piece, piece)
         mat_copies[p] = pltpu.make_async_copy(mat_hbm.at[rows], mat_ref.at[rows], local_sems.at[1 + p])
         mat_copies[p].start()
-
-    def at(dx=0, dzh=0, dy=0, zlow=zl):
-        return (((x + dx + 4) % 4) * 4 + (zh + dzh + 4) % 4, ((y + dy + 8) % 8) * 2 + zlow, l)
-
-    sibling = (r, c, 1 - l)
-    xup, xdown = at(dx=1), at(dx=-1)
-    device = {"zp": at(zlow=ol), "zo": at(dzh=-f, zlow=ol), "x": xup, "w": xdown, "yf": at(dy=f), "yn": at(dy=-f)}
-
-    barrier = pltpu.get_barrier_semaphore()
-    for other in (sibling, *device.values()):
-        pl.semaphore_signal(barrier, inc=1, device_id=other, device_id_type=MESH)
 
     column = 4 * c + lax.broadcasted_iota(jnp.int32, (1, tile), 1) // BLOCK
     own_left = 4 + zl

time: 68.9 us -> 68.9 us (level)
  no operation moved by 1% of the time
where the time goes in v5:
time: 68.9 us; the launch traced here: 68.1 us
  Pallas kernels  65.1 us (94%)
  local copies, waits for them, and re-layouts  2.29 us (3%)
    pallas_call x1, Pallas kernels, per_device(): pl.pallas_call(kernel, out_shape=(out, out), in_specs=[pl.BlockSpec(memor...  65.1 us
    unnamed x4, local copies, waits for them, and re-layouts  2.29 us

profile of v5, /device:TPU:1, one launch (start us, length us, event | category | flops | bytes accessed | tf_op | source)
XLA Modules:
  0.0 68.1 jit_solution(1232580102197947434)
XLA Ops:
  0.6 0.0 copy-start
  0.6 0.7 %copy-done = s32[64,17]{0,1:T(8,128)S(1)} copy-done((s32[64,17]{0,1:T(8,128)S(1)}, s32[64,17]{0,1:T(8,128)}, u32[]{:S(2)}) %copy-start) | copy-done | bytes 4376
  1.3 65.1 %shard_map.41 = (f32[512,256]{1,0:T(8,128)S(1)}, f32[512,256]{1,0:T(8,128)S(1)}) custom-call(s32[17,64]{1,0:T(8,128)S(1)} %bitcast.1, f32[512,512]{1,0:T(8,128)} %mat_hbm.1), custom_call_target="tpu_custom_call" | custom-call | flops 4000000000 | bytes 2097152 | tf_op jit(solution)/shard_map/pallas_call | solution.py:334
  66.5 0.8 %copy.6 = f32[512,256]{1,0:T(8,128)} copy(f32[512,256]{1,0:T(8,128)S(1)} %get-tuple-element.4) | data formatting | bytes 1048576
  67.3 0.8 %copy.7 = f32[512,256]{1,0:T(8,128)} copy(f32[512,256]{1,0:T(8,128)S(1)} %get-tuple-element.5) | data formatting | bytes 1048576
Async XLA Ops:
  0.6 0.7 %copy-start = (s32[64,17]{0,1:T(8,128)S(1)}, s32[64,17]{0,1:T(8,128)}, u32[]{:S(2)}) copy-start(s32[64,17]{0,1:T(8,128)} %param.3) | copy-start | bytes 13060

commit v6 on v4

--- a/solution.py
+++ b/solution.py
@@ -275,10 +275,7 @@
     def square_piece(a):
         rows = pl.ds(a * BLOCK, BLOCK)
         far_product(right, rows)
-        value = acc[rows, :] * mask_ref[pl.ds(a, 1), mine]
-        square_ref[rows, :] = value
-        cube[own_right, rows, :] = value.astype(jnp.bfloat16)
-        acc[rows, :] = jnp.zeros((BLOCK, width), jnp.float32)
+        cube[own_right, rows, :] = (acc[rows, :] * mask_ref[pl.ds(a, 1), mine]).astype(jnp.bfloat16)
 
     gather(right, right_recv, True, own_piece)
     acc[...] = jnp.zeros_like(acc)
@@ -300,6 +297,10 @@
 
     started = len(sent)
     gather(cube, cube_recv, False, square_piece)
+    for a in range(count):
+        rows = pl.ds(a * BLOCK, BLOCK)
+        square_ref[rows, :] = acc[rows, :] * mask_ref[pl.ds(a, 1), mine]
+        acc[rows, :] = jnp.zeros((BLOCK, width), jnp.float32)
     square_copy = pltpu.make_async_copy(square_ref, square_hbm, local_sems.at[0])
     square_copy.start()
     left_device(sent[:started])

time: 68.9 us -> 68.9 us (level)
  no operation moved by 1% of the time
where the time goes in v6:
time: 68.9 us; the launch traced here: 68.2 us
  Pallas kernels  65.2 us (95%)
  local copies, waits for them, and re-layouts  2.29 us (3%)
    pallas_call x1, Pallas kernels, per_device(): pl.pallas_call(kernel, out_shape=(out, out), in_specs=[pl.BlockSpec(memor...  65.2 us
    unnamed x4, local copies, waits for them, and re-layouts  2.29 us

profile of v6, /device:TPU:1, one launch (start us, length us, event | category | flops | bytes accessed | tf_op | source)
XLA Modules:
  0.0 68.2 jit_solution(5803921140346931112)
XLA Ops:
  0.6 0.0 copy-start
  0.6 0.7 %copy-done = s32[64,17]{0,1:T(8,128)S(1)} copy-done((s32[64,17]{0,1:T(8,128)S(1)}, s32[64,17]{0,1:T(8,128)}, u32[]{:S(2)}) %copy-start) | copy-done | bytes 4376
  1.3 65.2 %shard_map.41 = (f32[512,256]{1,0:T(8,128)S(1)}, f32[512,256]{1,0:T(8,128)S(1)}) custom-call(s32[17,64]{1,0:T(8,128)S(1)} %bitcast.1, f32[512,512]{1,0:T(8,128)} %mat_hbm.1), custom_call_target="tpu_custom_call" | custom-call | flops 4000000000 | bytes 2097152 | tf_op jit(solution)/shard_map/pallas_call | solution.py:336
  66.6 0.8 %copy.6 = f32[512,256]{1,0:T(8,128)} copy(f32[512,256]{1,0:T(8,128)S(1)} %get-tuple-element.4) | data formatting | bytes 1048576
  67.4 0.8 %copy.7 = f32[512,256]{1,0:T(8,128)} copy(f32[512,256]{1,0:T(8,128)S(1)} %get-tuple-element.5) | data formatting | bytes 1048576
Async XLA Ops:
  0.6 0.7 %copy-start = (s32[64,17]{0,1:T(8,128)S(1)}, s32[64,17]{0,1:T(8,128)}, u32[]{:S(2)}) copy-start(s32[64,17]{0,1:T(8,128)} %param.3) | copy-start | bytes 13060
